TPU v7x, 32 devices: a whole 2x2x4 slice. The times are simulated.
32 devices in a mesh: groups: 2 (over y), row: 4 (over z), col: 2 (over x), sub: 2 (over core).
Axes of the slice: x: 2, y: 2, z: 4, core: 2. Of those that a mesh axis runs over, the one named last changes fastest.
Arguments:
- orbital_factors: bfloat16 [2, 22528, 2048], P('sub', ('groups', 'col', 'row')), parts along dimension 1, may hold values from -0.8984375 to 0.8984375
- screen_mask: int32 [176, 2], P('groups'), parts along dimension 0, may hold values 0 or 1
Outputs:
- exchange_tiles: float32 [2, 11264, 11264], P(None, ('groups', 'row'), ('col', 'sub')), parts along dimension 1
There are 2 independent parts, one for each index of `groups`. A program takes and returns all parts, laid end to end along the dimension named above; each array names one. Nothing has to cross between parts.
All inputs are finite; a program needn't handle non-finite values.
Results may differ from a plain program's by a relative error of at most 0.0003.
Values may be sent and summed in bfloat16 or wider, within the bound.
No kernel may reach another device: no remote copies, remote signals or barrier semaphores. Data moves between devices by JAX's collectives and lax.ppermute only.
A program may use at most 256 MiB of HBM per device.

v0:
```python
import functools

import jax
import jax.numpy as jnp
from jax import lax
from jax.experimental import pallas as pl
from jax.experimental.pallas import tpu as pltpu
from jax.sharding import PartitionSpec as P

BLK = 128
AXES = ("row", "col", "sub")
MAX_GROUP = 88
VMEM_LIMIT = 63 * 2**20
TOKEN = (8, 128)


def apply_screen(panel, first_row, screen_mask, aux_start):
    row_total = panel.shape[1]
    block_ids = (first_row + jnp.arange(row_total, dtype=jnp.int32)) // BLK
    one_hot = (
        block_ids[:, None] == jnp.arange(screen_mask.shape[0], dtype=jnp.int32)[None, :]
    ).astype(jnp.float32)
    row_weights = jnp.dot(
        one_hot, screen_mask.astype(jnp.float32), preferred_element_type=jnp.float32
    )
    row_weights = lax.dynamic_slice_in_dim(row_weights, aux_start, panel.shape[0], 1)
    return panel * jnp.transpose(row_weights).astype(jnp.bfloat16)[:, :, None]


def gathered_shards(orbital_factors, screen_mask):
    aux_half, own_rows, occupied = orbital_factors.shape
    row_count = lax.axis_size("row")
    col_count = lax.axis_size("col")
    row_pos = lax.axis_index("row")
    col_pos = lax.axis_index("col")
    sub_pos = lax.axis_index("sub")
    own_first = (col_pos * row_count + row_pos) * own_rows
    screened = apply_screen(orbital_factors, own_first, screen_mask, sub_pos * aux_half)
    contract_dims = (((0, 2), (0, 2)), ((), ()))
    gathered_rows = lax.all_gather(screened, "col", axis=1, tiled=True)
    partial_tile = lax.dot_general(
        gathered_rows,
        lax.all_gather(screened, "row", axis=1, tiled=True),
        contract_dims,
        preferred_element_type=jnp.float32,
    )
    tile_sum = lax.psum_scatter(partial_tile, "sub", scatter_dimension=1, tiled=True)
    return tile_sum.reshape(col_count, own_rows, tile_sum.shape[1])


RESULT, CODED, ARRIVE, FAR, BASE1, BASE2, COLUMN, NEAR, FAR_INSIDE, CODED_NEAR = range(10)


def encode(acc, group):
    coded, exps = [], []
    for first in range(0, acc.shape[0], group):
        part = acc[first : first + group]
        top = jnp.max(jnp.abs(part), axis=0, keepdims=True)
        exp = jnp.floor(jnp.log2(jnp.maximum(top, 2.0**-100))) + 1.0
        scaled = jnp.round(part * jnp.exp2(15.0 - exp))
        coded.append(jnp.clip(scaled, -32767.0, 32767.0).astype(jnp.int32))
        exps.append(exp)
    return jnp.concatenate(coded, axis=0).astype(jnp.int16), exps


class Rows:
    def __init__(self, block, lo, count, cores):
        self.block, self.lo, self.count = block, lo, count
        self.mine = count // cores
        self.steps = 2 if self.mine < 1024 else 4
        self.tile = self.mine // self.steps
        self.group = max(g for g in range(8, MAX_GROUP + 1, 8) if self.tile % g == 0)


def exponent_rows(blocks):
    return -(-sum(r.mine // r.group for r in blocks) // 16) * 16


def overlap(segments, lo, hi):
    parts = []
    for k, (off, size) in enumerate(segments):
        first, last = max(lo, off), min(hi, off + size)
        if first < last:
            parts.append((k, first - off, last - first, first - lo))
    return parts


def target(flags, out, rows, lo, count, second, col, width):
    a = flags[COLUMN] if rows.block == 0 else 1 - flags[COLUMN]
    base = pl.multiple_of(flags[BASE2 if second else BASE1] + col, 128)
    return out.at[a, pl.ds(lo, count), pl.ds(base, width)]


def groups_of(send, blocks, pieces):
    if not send and len(blocks) == 1:
        return [(0, [p]) for p in range(len(pieces))]
    return [(b, list(range(len(pieces)))) for b in range(len(blocks))]


def locals_of(pieces):
    return [sum(n for _, _, n in pieces[:p]) for p in range(len(pieces))]


def mm_kernel(send, active, blocks, pieces, row_layout, col_layout, *refs):
    it = iter(refs)
    flags = next(it)
    next(it)
    rows = [[[next(it) for _ in range(2)] for _ in segments] for segments in row_layout]
    cols = [[[next(it) for _ in range(2)] for _ in sources] for sources in col_layout]
    rest = list(it)
    if send:
        out, token, rowbuf, colbuf, obuf, ebuf, ecode, rsem, csem, osem, esem = rest
    else:
        out, token, rowbuf, colbuf, obuf, rsem, csem, osem = rest[-8:]
    depth = rows[0][0][0].shape[1]
    begins = locals_of(pieces)
    firsts = [sum(r.mine for r in blocks[:b]) for b in range(len(blocks))]
    total = sum(r.mine for r in blocks)
    groups = groups_of(send, blocks, pieces)
    token[...] = jnp.zeros_like(token)

    def col_copy(p, aux, core):
        size = pieces[p][2]
        return pltpu.make_async_copy(
            cols[p][core][aux].at[pl.ds(col_layout[p][core][aux], size), :],
            colbuf.at[pl.ds(begins[p], size), pl.ds(aux * depth, depth)],
            csem.at[p, aux],
        )

    def row_copies(b, i, core):
        r = blocks[b]
        lo = r.lo + core * r.mine + i * r.tile
        spans = [(off, size) for off, size, _ in row_layout[b]]
        made = []
        for j, (k, off, size, local) in enumerate(overlap(spans, lo, lo + r.tile)):
            for aux in range(2):
                made.append(
                    pltpu.make_async_copy(
                        rows[b][k][aux].at[pl.ds(row_layout[b][k][2][aux] + off, size), :],
                        rowbuf.at[
                            pl.ds(firsts[b] + i * r.tile + local, size), pl.ds(aux * depth, depth)
                        ],
                        rsem.at[b, i, j, aux],
                    )
                )
        return made

    def per_core(act):
        for core in range(2):

            @pl.when(flags[FAR] == core)
            def _():
                act(core)

    def out_copies(g, i, slot):
        b, members = groups[g]
        r = blocks[b]
        if send:
            where = out.at[pl.ds(firsts[b] + i * r.tile, r.tile), :]
            return [pltpu.make_async_copy(obuf.at[slot, pl.ds(0, r.tile), :], where, osem.at[slot, 0])]
        made = []
        for p in members:
            second, off, n = pieces[p]
            where = target(flags, out, r, r.lo + i * r.tile, r.tile, second, off, n)
            source = obuf.at[slot, pl.ds(0, r.tile), pl.ds(begins[p] - begins[members[0]], n)]
            made.append(pltpu.make_async_copy(source, where, osem.at[slot, p]))
        return made

    def out_start(g, i, slot):
        for copy in out_copies(g, i, slot):
            copy.start()

    def out_wait(g, i, slot):
        for copy in out_copies(g, i, slot):
            copy.wait()

    def exp_copy():
        return pltpu.make_async_copy(
            ecode, out.at[pl.ds(total, exponent_rows(blocks)), :], esem.at[0]
        )

    @pl.when(flags[active] == 1)
    def _():
        def load(j):
            def begin(core):
                for aux in range(2):
                    col_copy(j, aux, core if len(cols[j]) > 1 else 0).start()

            if len(cols[j]) > 1:
                per_core(begin)
            else:
                begin(0)

        def load_rows(b, step):
            def begin(core):
                for copy in row_copies(b, step, core):
                    copy.start()

            if send:
                per_core(begin)
            else:
                begin(0)

        def wait_rows(b, step):
            def arrive(core):
                for copy in row_copies(b, step, core):
                    copy.wait()

            if send:
                per_core(arrive)
            else:
                arrive(0)

        def load_next(b, step):
            if step + 1 < blocks[b].steps:
                load_rows(b, step + 1)
            elif b + 1 < len(blocks):
                load_rows(b + 1, 0)

        def multiply(b, i, slot, local, size, place, scales):
            r = blocks[b]
            acc = lax.dot_general(
                rowbuf[pl.ds(pl.multiple_of(firsts[b] + i * r.tile, 16), r.tile), :],
                colbuf[pl.ds(local, size), :],
                (((1,), (1,)), ((), ())),
                preferred_element_type=jnp.float32,
            )
            if send:
                acc, exps = encode(acc, r.group)
                for g, exp in enumerate(exps):
                    pos = scales + i * (r.tile // r.group) + g
                    ebuf[pl.ds(pos, 1), pl.ds(local, size)] = exp
            obuf[slot, pl.ds(0, r.tile), pl.ds(place, size)] = acc

        load(0)
        load_rows(0, 0)
        for p in range(1, len(groups[0][1])):
            load(p)
        if send:
            ebuf[...] = jnp.zeros_like(ebuf)
        scales = 0
        for g, (b, members) in enumerate(groups):
            r = blocks[b]
            new_rows = g == 0 or groups[g - 1][0] != b
            new_cols = [p for p in members if all(p not in group[1] for group in groups[:g])]

            def body(i, carry, g=g, b=b, r=r, members=members, new_rows=new_rows, new_cols=new_cols, scales=scales):
                if new_rows:
                    for step in range(r.steps):

                        @pl.when(i == step)
                        def _(step=step):
                            wait_rows(b, step)
                            load_next(b, step)

                slot = lax.rem(i, 2)

                @pl.when(i >= 2)
                def _():
                    out_wait(g, i - 2, slot)

                if g > 0:

                    @pl.when(i < 2)
                    def _():
                        out_wait(g - 1, blocks[groups[g - 1][0]].steps - 2 + i, slot)

                for p in members:
                    if p in new_cols:

                        @pl.when(i == 0)
                        def _(p=p):
                            for aux in range(2):
                                col_copy(p, aux, 0).wait()
                            if g + 1 < len(groups) and p == new_cols[-1]:
                                for later in groups[g + 1][1]:
                                    if later not in members:
                                        load(later)

                    multiply(b, i, slot, begins[p], pieces[p][2], begins[p] - begins[members[0]], scales)
                out_start(g, i, slot)
                return carry

            lax.fori_loop(0, r.steps, body, 0)
            scales += r.mine // r.group
        if send:
            ecode[...] = ebuf[...].astype(jnp.int32).astype(jnp.int16)
            exp_copy().start()
        for slot in range(2):
            out_wait(len(groups) - 1, blocks[-1].steps - 2 + slot, slot)
        if send:
            exp_copy().wait()


def mm_call(flags, token, send, active, blocks, row_arrays, pieces, col_arrays, out, own_rows):
    width = sum(n for _, _, n in pieces)
    depth = row_arrays[0][0][2][0][0].shape[1]
    total = sum(r.mine for r in blocks)
    tile = max(r.tile for r in blocks)
    held = max(sum(pieces[p][2] for p in ps) for _, ps in groups_of(send, blocks, pieces))
    anywhere = pl.BlockSpec(memory_space=pltpu.HBM)
    operands = [flags, token]
    row_layout, col_layout = [], []
    for segments in row_arrays:
        row_layout.append([(off, size, tuple(b for _, b in halves)) for off, size, halves in segments])
        for _, _, halves in segments:
            operands += [array for array, _ in halves]
    for sources in col_arrays:
        col_layout.append([tuple(b for _, b in source) for source in sources])
        for source in sources:
            operands += [array for array, _ in source]
    in_specs = [pl.BlockSpec(memory_space=pltpu.SMEM)]
    in_specs += [anywhere] * (len(operands) - 1)
    aliases = {}
    scratch = [
        pltpu.VMEM((total, 2 * depth), jnp.bfloat16),
        pltpu.VMEM((width, 2 * depth), jnp.bfloat16),
        pltpu.VMEM((2, tile, held), jnp.int16 if send else jnp.float32),
    ]
    sems = [
        pltpu.SemaphoreType.DMA((len(blocks), max(r.steps for r in blocks), 4, 2)),
        pltpu.SemaphoreType.DMA((len(pieces), 2)),
        pltpu.SemaphoreType.DMA((2, len(pieces))),
    ]
    if send:
        exps = exponent_rows(blocks)
        out_shape = jax.ShapeDtypeStruct((total + exps, width), jnp.int16)
        scratch += [pltpu.VMEM((exps, width), jnp.float32), pltpu.VMEM((exps, width), jnp.int16)]
        sems += [pltpu.SemaphoreType.DMA((1,))]
    else:
        out_shape = jax.ShapeDtypeStruct((2, own_rows, 2 * own_rows), jnp.float32)
        if out is not None:
            operands.append(out)
            in_specs.append(anywhere)
            aliases = {len(operands) - 1: 0}
    return pl.pallas_call(
        functools.partial(mm_kernel, send, active, blocks, pieces, row_layout, col_layout),
        out_shape=(out_shape, jax.ShapeDtypeStruct(TOKEN, jnp.float32)),
        in_specs=in_specs,
        out_specs=(anywhere, pl.BlockSpec(memory_space=pltpu.VMEM)),
        scratch_shapes=scratch + sems,
        input_output_aliases=aliases,
        compiler_params=pltpu.CompilerParams(vmem_limit_bytes=VMEM_LIMIT),
        cost_estimate=pl.CostEstimate(flops=1, bytes_accessed=1, transcendentals=0),
        name="coded_tiles" if send else "result_tiles",
    )(*operands)


def decode_kernel(blocks, pieces, *refs):
    flags, _, *codes, _, out, token, qbuf, ebuf, obuf, qsem, esem, osem = refs
    exps = exponent_rows(blocks)
    cores = len(codes)
    width = sum(n for _, _, n in pieces)
    total = sum(r.mine for r in blocks)
    token[...] = jnp.zeros_like(token)
    work = []
    for core in range(cores):
        row, scale = 0, 0
        for r in blocks:
            for i in range(r.steps):
                work.append((core, r, row, r.lo + core * r.mine + i * r.tile, scale))
                row += r.tile
                scale += r.tile // r.group

    @pl.when(flags[ARRIVE] == 1)
    def _():
        def in_copy(j):
            core, r, row, _, _ = work[j]
            return pltpu.make_async_copy(
                codes[core].at[pl.ds(row, r.tile), :],
                qbuf.at[j, pl.ds(0, r.tile), :],
                qsem.at[j],
            )

        def exp_copy(core):
            return pltpu.make_async_copy(
                codes[core].at[pl.ds(total, exps), :], ebuf.at[core], esem.at[core]
            )

        def out_copy(j):
            _, r, _, lo, _ = work[j]
            return pltpu.make_async_copy(
                obuf.at[j % 2, pl.ds(0, r.tile), :],
                target(flags, out, r, lo, r.tile, *pieces[0][:2], width),
                osem.at[j % 2],
            )

        for core in range(cores):
            exp_copy(core).start()
        for j in range(len(work)):
            in_copy(j).start()
        scales = []
        for core in range(cores):
            exp_copy(core).wait()
            scales.append(jnp.exp2(ebuf[core].astype(jnp.int32).astype(jnp.float32) - 15.0))
        for j, (core, r, _, _, scale) in enumerate(work):
            in_copy(j).wait()
            if j >= 2:
                out_copy(j - 2).wait()
            values = qbuf[j, pl.ds(0, r.tile), :].astype(jnp.int32).astype(jnp.float32)
            for g in range(r.tile // r.group):
                obuf[j % 2, pl.ds(g * r.group, r.group), :] = (
                    values[g * r.group : (g + 1) * r.group] * scales[core][scale + g : scale + g + 1]
                )
            out_copy(j).start()
        for j in range(len(work) - 2, len(work)):
            out_copy(j).wait()


def decode_call(flags, token, coded, out, blocks, pieces):
    width = sum(n for _, _, n in pieces)
    tile = max(r.tile for r in blocks)
    count = len(coded) * sum(r.steps for r in blocks)
    anywhere = pl.BlockSpec(memory_space=pltpu.HBM)
    return pl.pallas_call(
        functools.partial(decode_kernel, blocks, pieces),
        out_shape=(
            jax.ShapeDtypeStruct(out.shape, out.dtype),
            jax.ShapeDtypeStruct(TOKEN, jnp.float32),
        ),
        in_specs=[pl.BlockSpec(memory_space=pltpu.SMEM)] + [anywhere] * (2 + len(coded)),
        out_specs=(anywhere, pl.BlockSpec(memory_space=pltpu.VMEM)),
        scratch_shapes=[
            pltpu.VMEM((count, tile, width), jnp.int16),
            pltpu.VMEM((len(coded), exponent_rows(blocks), width), jnp.int16),
            pltpu.VMEM((2, tile, width), jnp.float32),
            pltpu.SemaphoreType.DMA((count,)),
            pltpu.SemaphoreType.DMA((2,)),
            pltpu.SemaphoreType.DMA((2,)),
        ],
        input_output_aliases={2 + len(coded): 0},
        compiler_params=pltpu.CompilerParams(vmem_limit_bytes=VMEM_LIMIT),
        cost_estimate=pl.CostEstimate(flops=1, bytes_accessed=1, transcendentals=0),
        name="decode_tiles",
    )(flags, token, *coded, out)


def permute(value, move):
    pairs = []
    for r in range(4):
        for c in range(2):
            for s in range(2):
                to = move(r, c, s)
                if to is not None:
                    pairs.append(((r * 2 + c) * 2 + s, (to[0] * 2 + to[1]) * 2 + to[2]))
    return lax.ppermute(value, AXES, pairs)


def inner(r):
    return r in (1, 2)


def far_core(r):
    return 1 - r // 2


def symmetric_shards(chunks, orbital_factors, screen_mask):
    _, own_rows, occupied = orbital_factors.shape
    r, c, s = (lax.axis_index(name) for name in AXES)
    side = r // 2
    t = s ^ side
    inside = jnp.logical_and(r >= 1, r <= 2)
    near = t == 0
    flags = jnp.stack(
        [
            jnp.logical_or(near, inside).astype(jnp.int32),
            inside.astype(jnp.int32),
            jnp.logical_and(jnp.logical_not(near), jnp.logical_not(inside)).astype(jnp.int32),
            t.astype(jnp.int32),
            (jnp.where(near, 1 - r % 2, side) * own_rows).astype(jnp.int32),
            (jnp.where(near, r % 2, 1 - side) * own_rows).astype(jnp.int32),
            c.astype(jnp.int32),
            near.astype(jnp.int32),
            jnp.logical_and(jnp.logical_not(near), inside).astype(jnp.int32),
            jnp.logical_and(near, inside).astype(jnp.int32),
        ]
    )
    per_block = own_rows // BLK
    weights = lax.dynamic_slice(screen_mask, ((c * 4 + r) * per_block, s), (per_block, 1))
    weights = weights.astype(jnp.bfloat16)
    def mask(off, size):
        part = orbital_factors[0, off : off + size].reshape(size // BLK, BLK, occupied)
        part = part * weights[off // BLK : (off + size) // BLK][:, :, None]
        return part.reshape(size, occupied)

    outer_pair = lambda r, c, s: (r ^ 1, c, s)
    mid_pair = lambda r, c, s: (3 - r, c, s) if inner(r) else None
    x_pair = lambda r, c, s: (r, 1 - c, s)
    x_inner = lambda r, c, s: (r, 1 - c, s) if inner(r) else None
    swap = lambda r, c, s: (r, c, 1 - s)
    near_to_far = lambda r, c, s: (r ^ 1, c, 1 - s) if inner(r) and far_core(r) != s else None
    far_to_far = lambda r, c, s: (r ^ 1, c, s) if inner(r) and far_core(r) == s else None

    state = {"out": None, "token": jnp.zeros(TOKEN, jnp.float32)}
    arrays = {}
    moves = {
        "nb": outer_pair, "m1": mid_pair, "m2": mid_pair, "rx": x_pair, "nbx": x_inner,
        "n": near_to_far, "f": far_to_far,
    }
    sources = {"nb": "part", "m1": "part", "rx": "part", "m2": "nb", "nbx": "nb", "n": "code", "f": "code"}

    def tie(value):
        value, state["token"] = lax.optimization_barrier((value, state["token"]))
        return value

    def start(kind, k):
        arrays[kind, k] = permute(tie(arrays[sources[kind], k]), moves[kind])

    def done(kind, k):
        arrays[kind, k] = tie(arrays[kind, k])

    def start_swap(kind, k):
        arrays[kind + "_h", k] = permute(tie(arrays[kind, k]), swap)

    def done_swap(kind, k):
        arrays[kind + "_h", k] = tie(arrays[kind + "_h", k])


    def halves(kind, k):
        return (arrays[kind, k], 0), (arrays[kind + "_h", k], 0)

    def rows_of(kinds, cores):
        blocks, segments = [], []
        for kind, which in kinds:
            lo = chunks[which[0]][0]
            count = sum(chunks[k][1] for k in which)
            blocks.append(Rows(int(kind in ("nbx", "rx")), lo, count, cores))
            segments.append([(*chunks[k], halves(kind, k)) for k in which])
        return blocks, segments

    def pieces_of(where):
        return [(second, *chunks[k]) for second, k in where]

    def coded(name, kinds, *where, cores=2):
        blocks, rows = rows_of(kinds, cores)
        cols = [[halves(("m1", "m2")[second], k)] for second, k in where]
        arrays["code", name], state["token"] = mm_call(
            flags, state["token"], True, CODED if cores == 2 else CODED_NEAR, blocks, rows,
            pieces_of(where), cols, None, own_rows,
        )
        arrays["item", name] = (blocks, pieces_of(where))

    def result(kinds, *where, active=RESULT):
        blocks, rows = rows_of(kinds, 1)
        names = (("nb", "m1"), {RESULT: ("own", "m2"), NEAR: ("own",), FAR_INSIDE: ("m2",)}[active])
        cols = [[halves(kind, k) for kind in names[second]] for second, k in where]
        state["out"], state["token"] = mm_call(
            flags, state["token"], False, active, blocks, rows, pieces_of(where), cols, state["out"],
            own_rows,
        )

    def decode(name):
        state["out"], state["token"] = decode_call(
            flags, state["token"], [arrays[kind, name] for kind in "nf" if (kind, name) in arrays],
            state["out"], *arrays["item", name],
        )

    for k, chunk in enumerate(chunks):
        arrays["part", k] = arrays["own", k] = mask(*chunk)
    both = [0, 1]

    start("nb", 0)
    start("m1", 0)
    start("rx", 0)
    start_swap("own", 0)
    start_swap("own", 1)
    done_swap("own", 0)
    done_swap("own", 1)
    done("nb", 0)
    done("m1", 0)
    done("rx", 0)
    start("nb", 1)
    start("m1", 1)
    start("nbx", 0)
    start_swap("nb", 0)
    start_swap("m1", 0)
    start_swap("rx", 0)
    done_swap("nb", 0)
    done_swap("m1", 0)
    done_swap("rx", 0)
    result([("own", both), ("rx", [0])], (0, 0))
    result([("own", both)], (1, 0), (1, 1), active=NEAR)
    done("nb", 1)
    done("m1", 1)
    done("nbx", 0)
    start("m2", 1)
    start("nbx", 1)
    start_swap("nb", 1)
    start_swap("m1", 1)
    start_swap("nbx", 0)
    done_swap("nb", 1)
    done_swap("m1", 1)
    done_swap("nbx", 0)
    coded(0, [("nb", both)], (0, 0), (0, 1))
    start("n", 0)
    start("f", 0)
    coded(1, [("nbx", [0])], (0, 0), (0, 1))
    result([("own", both), ("rx", [0])], (0, 1))
    done("m2", 1)
    done("nbx", 1)
    done("n", 0)
    done("f", 0)
    start("m2", 0)
    start("n", 1)
    start("f", 1)
    start_swap("m2", 1)
    start_swap("nbx", 1)
    done_swap("m2", 1)
    done_swap("nbx", 1)
    start("rx", 1)
    coded(2, [("nbx", [1])], (0, 0), (0, 1))
    done("n", 1)
    done("f", 1)
    start("n", 2)
    start("f", 2)
    coded(3, [("nb", both), ("nbx", both)], (1, 1))
    done("m2", 0)
    done("n", 2)
    done("f", 2)
    start("n", 3)
    start("f", 3)
    start_swap("m2", 0)
    done_swap("m2", 0)
    coded(4, [("nb", both), ("nbx", both)], (1, 0), cores=1)
    result([("rx", [0])], (1, 0), (1, 1), active=NEAR)
    result([("own", both), ("rx", [0])], (1, 1), active=FAR_INSIDE)
    result([("own", both), ("rx", [0])], (1, 0), active=FAR_INSIDE)
    done("n", 3)
    done("f", 3)
    start("n", 4)
    done("rx", 1)
    start_swap("rx", 1)
    for name in range(4):
        decode(name)
    done_swap("rx", 1)
    result([("rx", [1])], (0, 0), (0, 1), (1, 1), (1, 0))
    decode(4)
    return state["out"]


def split_rows(own_rows):
    size = own_rows // BLK // 2 * BLK
    return [(0, size), (size, own_rows - size)]


def solution(mesh):
    placed = (P("sub", ("groups", "col", "row"), None), P("groups", None))
    result = P(None, ("groups", "row"), ("col", "sub"))

    def shards(orbital_factors, screen_mask):
        aux_half, own_rows, _ = orbital_factors.shape
        small = (mesh.shape["row"], mesh.shape["col"], mesh.shape["sub"]) == (4, 2, 2)
        if small and aux_half == 1 and own_rows == 11 * BLK:
            return symmetric_shards(split_rows(own_rows), orbital_factors, screen_mask)
        return gathered_shards(orbital_factors, screen_mask)

    return jax.shard_map(
        shards, mesh=mesh, in_specs=placed, out_specs=result, check_vma=False
    )
```

profile of v0, /device:TPU:1, one launch (start us, length us, event | category | flops | bytes accessed | tf_op | source)
XLA Modules:
  0.0 390.1 jit_solution(4720862692838444121)
XLA Ops:
  0.9 2.0 bitcast_multiply_fusion.1.refs_2_.refs_6_.refs_4_.refs_16_
  3.0 4.7 %bitcast_multiply_fusion.refs_4_.refs_8_.refs_6_.refs_12_ = bf16[768,2048]{1,0:T(8,128)(2,1)} fusion(bf16[1,1408,2048]{2,1,0:T(8,128)(2,1)} %param.2, bf16[768]{0:T(1024)(128)(2,1)S(1)} %broadcast_bitcast_fusion.1), kind=kLoop, calls=%fused_computation | loop fusion | flops 1572864 | bytes 6292992 | tf_op jit(solution)/shard_map/mul | solution.py:483
  8.1 2.3 collective-permute-start.2
  10.4 2.1 collective-permute-start.1
  13.8 3.1 collective-permute-done.4.refs_3_.refs_7_.refs_5_.refs_17_
  17.3 50.1 %collective-permute-done.2.refs_8_.refs_2_.refs_4_ = bf16[640,2048]{1,0:T(8,128)(2,1)} collective-permute-done((bf16[640,2048]{1,0:T(8,128)(2,1)S(1)}, bf16[640,2048]{1,0:T(8,128)(2,1)}, u32[]{:S(2)}, u32[]{:S(2)}) %collective-permute-start.2) | collective-permute-done | bytes 2621472 | tf_op jit(solution)/shard_map/ppermute | solution.py:446
  67.3 2.8 collective-permute-done.refs_6_.refs_2_
  70.2 1.7 collective-permute-start.8
  71.9 2.5 collective-permute-start.5
  74.3 2.3 collective-permute-start.10
  77.2 2.1 collective-permute-start.9
  79.9 4.0 %collective-permute-done.7.refs_11_.refs_7_.refs_5_ = bf16[640,2048]{1,0:T(8,128)(2,1)} collective-permute-done((bf16[640,2048]{1,0:T(8,128)(2,1)}, bf16[640,2048]{1,0:T(8,128)(2,1)}, u32[]{:S(2)}, u32[]{:S(2)}) %collective-permute-start.7) | collective-permute-done | bytes 2621472 | tf_op jit(solution)/shard_map/ppermute | solution.py:446
  83.9 1.5 collective-permute-done.6.refs_7_.refs_3_
  86.0 1.9 result_tiles.7
  87.9 1.6 result_tiles.8
  89.5 53.5 %collective-permute-done.5.refs_4_.refs_8_ = bf16[768,2048]{1,0:T(8,128)(2,1)} collective-permute-done((bf16[768,2048]{1,0:T(8,128)(2,1)}, bf16[768,2048]{1,0:T(8,128)(2,1)}, u32[]{:S(2)}, u32[]{:S(2)}) %collective-permute-start.5) | collective-permute-done | bytes 3145760 | tf_op jit(solution)/shard_map/ppermute | solution.py:446
  144.2 2.4 collective-permute-start.12
  146.6 2.3 collective-permute-start.11
  149.3 4.5 %collective-permute-done.14.refs_9_.refs_7_.refs_11_ = bf16[768,2048]{1,0:T(8,128)(2,1)} collective-permute-done((bf16[768,2048]{1,0:T(8,128)(2,1)}, bf16[768,2048]{1,0:T(8,128)(2,1)}, u32[]{:S(2)}, u32[]{:S(2)}) %collective-permute-start.14) | collective-permute-done | bytes 3145760 | tf_op jit(solution)/shard_map/ppermute | solution.py:446
  153.8 3.7 collective-permute-done.13.refs_3_.refs_7_
  157.6 2.0 coded_tiles.5
  159.5 1.3 collective-permute-start.17
  160.8 1.3 collective-permute-start.16
  162.1 1.5 coded_tiles.6
  163.6 1.9 result_tiles.9
  165.5 58.9 %collective-permute-done.17.refs_2_ = s16[720,1408]{1,0:T(8,128)(2,1)} collective-permute-done((s16[720,1408]{1,0:T(8,128)(2,1)}, s16[720,1408]{1,0:T(8,128)(2,1)}, u32[]{:S(2)}, u32[]{:S(2)}) %collective-permute-start.17) | collective-permute-done | bytes 2027552 | tf_op jit(solution)/shard_map/ppermute | solution.py:446
  224.4 2.4 collective-permute-done.16.refs_3_
  227.3 2.1 collective-permute-start.21
  230.7 1.5 collective-permute-start.22
  232.8 4.5 %collective-permute-done.18.refs_3_.refs_9_ = bf16[768,2048]{1,0:T(8,128)(2,1)} collective-permute-done((bf16[768,2048]{1,0:T(8,128)(2,1)}, bf16[768,2048]{1,0:T(8,128)(2,1)}, u32[]{:S(2)}, u32[]{:S(2)}) %collective-permute-start.18) | collective-permute-done | bytes 3145760 | tf_op jit(solution)/shard_map/ppermute | solution.py:446
  237.3 1.5 coded_tiles.7
  238.8 15.7 %collective-permute-done.23.refs_2_ = s16[336,1408]{1,0:T(8,128)(2,1)S(1)} collective-permute-done((s16[336,1408]{1,0:T(8,128)(2,1)}, s16[336,1408]{1,0:T(8,128)(2,1)S(1)}, u32[]{:S(2)}, u32[]{:S(2)}) %collective-permute-start.23) | collective-permute-done | bytes 946208 | tf_op jit(solution)/shard_map/ppermute | solution.py:446
  259.1 1.6 coded_tiles.8
  260.7 23.4 %collective-permute-done.25.refs_2_ = s16[400,1408]{1,0:T(8,128)(2,1)} collective-permute-done((s16[400,1408]{1,0:T(8,128)(2,1)}, s16[400,1408]{1,0:T(8,128)(2,1)}, u32[]{:S(2)}, u32[]{:S(2)}) %collective-permute-start.25) | collective-permute-done | bytes 1126432 | tf_op jit(solution)/shard_map/ppermute | solution.py:446
  287.4 2.7 collective-permute-done.26.refs_11_.refs_9_.refs_19_
  290.1 1.9 coded_tiles.9
  291.9 1.7 result_tiles.10
  293.6 1.9 result_tiles.11
  295.5 1.9 result_tiles.12
  297.4 38.7 %collective-permute-done.28.refs_2_ = s16[1424,768]{1,0:T(8,128)(2,1)} collective-permute-done((s16[1424,768]{1,0:T(8,128)(2,1)}, s16[1424,768]{1,0:T(8,128)(2,1)}, u32[]{:S(2)}, u32[]{:S(2)}) %collective-permute-start.28) | collective-permute-done | bytes 2187296 | tf_op jit(solution)/shard_map/ppermute | solution.py:446
  336.1 1.9 collective-permute-done.27.refs_3_
  339.3 7.0 %decode_tiles.5 = (f32[2,1408,2816]{2,1,0:T(8,128)}, f32[8,128]{1,0:T(8,128)}) custom-call(s32[10]{0:T(128)} %stack.67.refs_0_, f32[8,128]{1,0:T(8,128)} %get-tuple-element.286.refs_1_, s16[720,1408]{1,0:T(8,128)(2,1)} %collective-permute-done.17.refs_2_, s16[720,1408]{1,0:T(8,128)(2,1)} %collective-permute-done.16.refs_3_, ...), custom_call_target="tpu_custom_call", output_to_operand_aliasing={{0}: (4, {})} | custom-call | flops 1 | bytes 1 | tf_op jit(solution)/shard_map/decode_tiles/pallas_call | solution.py:415
  346.3 4.9 %decode_tiles.6 = (f32[2,1408,2816]{2,1,0:T(8,128)}, f32[8,128]{1,0:T(8,128)}) custom-call(s32[10]{0:T(128)} %stack.67.refs_0_, f32[8,128]{1,0:T(8,128)} %get-tuple-element.290.refs_1_, s16[336,1408]{1,0:T(8,128)(2,1)} %copy-done.4, s16[336,1408]{1,0:T(8,128)(2,1)} %collective-permute-done.22.refs_3_, ...), custom_call_target="tpu_custom_call", output_to_operand_aliasing={{0}: (4, {})} | custom-call | flops 1 | bytes 1 | tf_op jit(solution)/shard_map/decode_tiles/pallas_call | solution.py:415
  351.2 5.2 %decode_tiles.7 = (f32[2,1408,2816]{2,1,0:T(8,128)}, f32[8,128]{1,0:T(8,128)}) custom-call(s32[10]{0:T(128)} %stack.67.refs_0_, f32[8,128]{1,0:T(8,128)} %get-tuple-element.294.refs_1_, s16[400,1408]{1,0:T(8,128)(2,1)} %collective-permute-done.25.refs_2_, s16[400,1408]{1,0:T(8,128)(2,1)} %collective-permute-done.24.refs_3_, ...), custom_call_target="tpu_custom_call", output_to_operand_aliasing={{0}: (4, {})} | custom-call | flops 1 | bytes 1 | tf_op jit(solution)/shard_map/decode_tiles/pallas_call | solution.py:415
  356.4 8.0 %decode_tiles.8 = (f32[2,1408,2816]{2,1,0:T(8,128)}, f32[8,128]{1,0:T(8,128)}) custom-call(s32[10]{0:T(128)} %stack.67.refs_0_, f32[8,128]{1,0:T(8,128)} %get-tuple-element.298.refs_1_, s16[1424,768]{1,0:T(8,128)(2,1)} %collective-permute-done.28.refs_2_, s16[1424,768]{1,0:T(8,128)(2,1)} %collective-permute-done.27.refs_3_, ...), custom_call_target="tpu_custom_call", output_to_operand_aliasing={{0}: (4, {})} | custom-call | flops 1 | bytes 1 | tf_op jit(solution)/shard_map/decode_tiles/pallas_call | solution.py:415
  364.4 1.6 result_tiles.13
  366.0 16.2 %collective-permute-done.30.refs_2_ = s16[2848,640]{1,0:T(8,128)(2,1)} collective-permute-done((s16[2848,640]{1,0:T(8,128)(2,1)}, s16[2848,640]{1,0:T(8,128)(2,1)}, u32[]{:S(2)}, u32[]{:S(2)}) %collective-permute-start.30) | collective-permute-done | bytes 3645472 | tf_op jit(solution)/shard_map/ppermute | solution.py:446
  382.2 7.4 %decode_tiles.9 = (f32[2,1408,2816]{2,1,0:T(8,128)}, f32[8,128]{1,0:T(8,128)}) custom-call(s32[10]{0:T(128)} %stack.67.refs_0_, f32[8,128]{1,0:T(8,128)} %get-tuple-element.307.refs_1_, s16[2848,640]{1,0:T(8,128)(2,1)} %collective-permute-done.30.refs_2_, f32[2,1408,2816]{2,1,0:T(8,128)} %get-tuple-element.309.refs_3_), custom_call_target="tpu_custom_call", output_to_operand_aliasing={{0}: (3, {})} | custom-call | flops 1 | bytes 1 | tf_op jit(solution)/shard_map/decode_tiles/pallas_call | solution.py:415
  (50 shorter events, 18.0 us)
Async XLA Ops:
  2.9 9.7 %copy-start = (bf16[640,2048]{1,0:T(8,128)(2,1)}, bf16[640,2048]{1,0:T(8,128)(2,1)S(1)}, u32[]{:S(2)}) copy-start(bf16[640,2048]{1,0:T(8,128)(2,1)S(1)} %bitcast_multiply_fusion.1.refs_2_.refs_6_.refs_4_.refs_16_) | copy-start | bytes 7864324
  7.6 9.6 %collective-permute-start.3 = (bf16[768,2048]{1,0:T(8,128)(2,1)}, bf16[768,2048]{1,0:T(8,128)(2,1)S(1)}, u32[]{:S(2)}, u32[]{:S(2)}) collective-permute-start(bf16[768,2048]{1,0:T(8,128)(2,1)} %bitcast_multiply_fusion.refs_4_.refs_8_.refs_6_.refs_12_), channel_id=1, source_target_pairs={{0,1},{1,0},{2,3},{3,2},{4,5},{5,4},{6,7},{7,6},{8,9},{9,8},{10,11... | collective-permute-start | bytes 9437192 | tf_op jit(solution)/shard_map/ppermute | solution.py:446
  7.7 9.2 %collective-permute-start.4 = (bf16[640,2048]{1,0:T(8,128)(2,1)S(1)}, bf16[640,2048]{1,0:T(8,128)(2,1)S(1)}, u32[]{:S(2)}, u32[]{:S(2)}) collective-permute-start(bf16[640,2048]{1,0:T(8,128)(2,1)S(1)} %bitcast_multiply_fusion.1.refs_2_.refs_6_.refs_4_.refs_16_), channel_id=1, source_target_pairs={{0,1},{1,0},{2,3},{3,2},{4,5},{5,4},{6,7},{7,6},{8,9},{9,8},{10,11... | collective-permute-start | bytes 7864328 | tf_op jit(solution)/shard_map/ppermute | solution.py:446
  8.1 59.2 %collective-permute-start.2 = (bf16[640,2048]{1,0:T(8,128)(2,1)S(1)}, bf16[640,2048]{1,0:T(8,128)(2,1)}, u32[]{:S(2)}, u32[]{:S(2)}) collective-permute-start(bf16[640,2048]{1,0:T(8,128)(2,1)S(1)} %bitcast_multiply_fusion.1.refs_2_.refs_6_.refs_4_.refs_16_), channel_id=1, source_target_pairs={{0,4},{1,5},{2,6},{3,7},{4,0},{5,1},{6,2},{7,3},{8,12},{9,13},{10,... | collective-permute-start | bytes 7864328 | tf_op jit(solution)/shard_map/ppermute | solution.py:446
  10.4 56.9 %collective-permute-start.1 = (bf16[640,2048]{1,0:T(8,128)(2,1)S(1)}, bf16[640,2048]{1,0:T(8,128)(2,1)}, u32[]{:S(2)}, u32[]{:S(2)}) collective-permute-start(bf16[640,2048]{1,0:T(8,128)(2,1)S(1)} %bitcast_multiply_fusion.1.refs_2_.refs_6_.refs_4_.refs_16_), channel_id=1, source_target_pairs={{4,8},{5,9},{6,10},{7,11},{8,4},{9,5},{10,6},{11,7},{20,24},{21,25... | collective-permute-start | bytes 7864328 | tf_op jit(solution)/shard_map/ppermute | solution.py:446
  12.6 57.6 %collective-permute-start = (bf16[640,2048]{1,0:T(8,128)(2,1)S(1)}, bf16[640,2048]{1,0:T(8,128)(2,1)S(1)}, u32[]{:S(2)}, u32[]{:S(2)}) collective-permute-start(bf16[640,2048]{1,0:T(8,128)(2,1)S(1)} %bitcast_multiply_fusion.1.refs_2_.refs_6_.refs_4_.refs_16_), channel_id=1, source_target_pairs={{0,2},{1,3},{2,0},{3,1},{4,6},{5,7},{6,4},{7,5},{8,10},{9,11},{10,... | collective-permute-start | bytes 7864328 | tf_op jit(solution)/shard_map/ppermute | solution.py:446
  16.9 55.0 %copy-start.2 = (bf16[640,2048]{1,0:T(8,128)(2,1)}, bf16[640,2048]{1,0:T(8,128)(2,1)S(1)}, u32[]{:S(2)}) copy-start(bf16[640,2048]{1,0:T(8,128)(2,1)S(1)} %collective-permute-done.4.refs_3_.refs_7_.refs_5_.refs_17_) | copy-start | bytes 7864324
  17.3 52.9 %copy-start.1 = (bf16[768,2048]{1,0:T(8,128)(2,1)}, bf16[768,2048]{1,0:T(8,128)(2,1)S(1)}, u32[]{:S(2)}) copy-start(bf16[768,2048]{1,0:T(8,128)(2,1)S(1)} %collective-permute-done.3.refs_5_.refs_9_.refs_7_.refs_13_) | copy-start | bytes 9437188
  70.2 6.8 %copy-start.3 = (bf16[640,2048]{1,0:T(8,128)(2,1)}, bf16[640,2048]{1,0:T(8,128)(2,1)S(1)}, u32[]{:S(2)}) copy-start(bf16[640,2048]{1,0:T(8,128)(2,1)S(1)} %collective-permute-done.refs_6_.refs_2_) | copy-start | bytes 7864324
  70.2 7.0 %collective-permute-start.8 = (bf16[640,2048]{1,0:T(8,128)(2,1)}, bf16[640,2048]{1,0:T(8,128)(2,1)}, u32[]{:S(2)}, u32[]{:S(2)}) collective-permute-start(bf16[640,2048]{1,0:T(8,128)(2,1)} %collective-permute-done.2.refs_8_.refs_2_.refs_4_), channel_id=1, source_target_pairs={{0,1},{1,0},{2,3},{3,2},{4,5},{5,4},{6,7},{7,6},{8,9},{9,8},{10,11... | collective-permute-start | bytes 7864328 | tf_op jit(solution)/shard_map/ppermute | solution.py:446
  71.9 71.2 %collective-permute-start.5 = (bf16[768,2048]{1,0:T(8,128)(2,1)}, bf16[768,2048]{1,0:T(8,128)(2,1)}, u32[]{:S(2)}, u32[]{:S(2)}) collective-permute-start(bf16[768,2048]{1,0:T(8,128)(2,1)} %bitcast_multiply_fusion.refs_4_.refs_8_.refs_6_.refs_12_), channel_id=1, source_target_pairs={{0,4},{1,5},{2,6},{3,7},{4,0},{5,1},{6,2},{7,3},{8,12},{9,13},{10,... | collective-permute-start | bytes 9437192 | tf_op jit(solution)/shard_map/ppermute | solution.py:446
  74.3 68.7 %collective-permute-start.10 = (bf16[768,2048]{1,0:T(8,128)(2,1)}, bf16[768,2048]{1,0:T(8,128)(2,1)}, u32[]{:S(2)}, u32[]{:S(2)}) collective-permute-start(bf16[768,2048]{1,0:T(8,128)(2,1)} %bitcast_multiply_fusion.refs_4_.refs_8_.refs_6_.refs_12_), channel_id=1, source_target_pairs={{4,8},{5,9},{6,10},{7,11},{8,4},{9,5},{10,6},{11,7},{20,24},{21,25... | collective-permute-start | bytes 9437192 | tf_op jit(solution)/shard_map/ppermute | solution.py:446
  76.6 7.3 %collective-permute-start.7 = (bf16[640,2048]{1,0:T(8,128)(2,1)}, bf16[640,2048]{1,0:T(8,128)(2,1)}, u32[]{:S(2)}, u32[]{:S(2)}) collective-permute-start(bf16[640,2048]{1,0:T(8,128)(2,1)} %collective-permute-done.1.refs_10_.refs_6_.refs_4_), channel_id=1, source_target_pairs={{0,1},{1,0},{2,3},{3,2},{4,5},{5,4},{6,7},{7,6},{8,9},{9,8},{10,11... | collective-permute-start | bytes 7864328 | tf_op jit(solution)/shard_map/ppermute | solution.py:446
  77.0 8.4 %collective-permute-start.6 = (bf16[640,2048]{1,0:T(8,128)(2,1)S(1)}, bf16[640,2048]{1,0:T(8,128)(2,1)}, u32[]{:S(2)}, u32[]{:S(2)}) collective-permute-start(bf16[640,2048]{1,0:T(8,128)(2,1)S(1)} %collective-permute-done.refs_6_.refs_2_), channel_id=1, source_target_pairs={{0,1},{1,0},{2,3},{3,2},{4,5},{5,4},{6,7},{7,6},{8,9},{9,8},{10,11... | collective-permute-start | bytes 7864328 | tf_op jit(solution)/shard_map/ppermute | solution.py:446
  77.2 65.9 %collective-permute-start.9 = (bf16[640,2048]{1,0:T(8,128)(2,1)}, bf16[640,2048]{1,0:T(8,128)(2,1)}, u32[]{:S(2)}, u32[]{:S(2)}) collective-permute-start(bf16[640,2048]{1,0:T(8,128)(2,1)} %collective-permute-done.2.refs_8_.refs_2_.refs_4_), channel_id=1, source_target_pairs={{4,6},{5,7},{6,4},{7,5},{8,10},{9,11},{10,8},{11,9},{20,22},{21,23... | collective-permute-start | bytes 7864328 | tf_op jit(solution)/shard_map/ppermute | solution.py:446
  143.0 6.3 %collective-permute-start.15 = (bf16[768,2048]{1,0:T(8,128)(2,1)}, bf16[768,2048]{1,0:T(8,128)(2,1)}, u32[]{:S(2)}, u32[]{:S(2)}) collective-permute-start(bf16[768,2048]{1,0:T(8,128)(2,1)} %collective-permute-done.5.refs_4_.refs_8_), channel_id=1, source_target_pairs={{0,1},{1,0},{2,3},{3,2},{4,5},{5,4},{6,7},{7,6},{8,9},{9,8},{10,11... | collective-permute-start | bytes 9437192 | tf_op jit(solution)/shard_map/ppermute | solution.py:446
  143.7 10.1 %collective-permute-start.14 = (bf16[768,2048]{1,0:T(8,128)(2,1)}, bf16[768,2048]{1,0:T(8,128)(2,1)}, u32[]{:S(2)}, u32[]{:S(2)}) collective-permute-start(bf16[768,2048]{1,0:T(8,128)(2,1)} %collective-permute-done.10.refs_8_.refs_6_.refs_10_), channel_id=1, source_target_pairs={{0,1},{1,0},{2,3},{3,2},{4,5},{5,4},{6,7},{7,6},{8,9},{9,8},{10,11... | collective-permute-start | bytes 9437192 | tf_op jit(solution)/shard_map/ppermute | solution.py:446
  143.8 13.8 %collective-permute-start.13 = (bf16[640,2048]{1,0:T(8,128)(2,1)}, bf16[640,2048]{1,0:T(8,128)(2,1)}, u32[]{:S(2)}, u32[]{:S(2)}) collective-permute-start(bf16[640,2048]{1,0:T(8,128)(2,1)} %collective-permute-done.9.refs_2_.refs_6_), channel_id=1, source_target_pairs={{0,1},{1,0},{2,3},{3,2},{4,5},{5,4},{6,7},{7,6},{8,9},{9,8},{10,11... | collective-permute-start | bytes 7864328 | tf_op jit(solution)/shard_map/ppermute | solution.py:446
  144.2 21.3 %collective-permute-start.12 = (bf16[768,2048]{1,0:T(8,128)(2,1)}, bf16[768,2048]{1,0:T(8,128)(2,1)}, u32[]{:S(2)}, u32[]{:S(2)}) collective-permute-start(bf16[768,2048]{1,0:T(8,128)(2,1)} %collective-permute-done.5.refs_4_.refs_8_), channel_id=1, source_target_pairs={{4,8},{5,9},{6,10},{7,11},{8,4},{9,5},{10,6},{11,7},{20,24},{21,25... | collective-permute-start | bytes 9437192 | tf_op jit(solution)/shard_map/ppermute | solution.py:446
  146.6 18.9 %collective-permute-start.11 = (bf16[768,2048]{1,0:T(8,128)(2,1)}, bf16[768,2048]{1,0:T(8,128)(2,1)}, u32[]{:S(2)}, u32[]{:S(2)}) collective-permute-start(bf16[768,2048]{1,0:T(8,128)(2,1)} %collective-permute-done.5.refs_4_.refs_8_), channel_id=1, source_target_pairs={{4,6},{5,7},{6,4},{7,5},{8,10},{9,11},{10,8},{11,9},{20,22},{21,23... | collective-permute-start | bytes 9437192 | tf_op jit(solution)/shard_map/ppermute | solution.py:446
  159.5 64.9 %collective-permute-start.17 = (s16[720,1408]{1,0:T(8,128)(2,1)}, s16[720,1408]{1,0:T(8,128)(2,1)}, u32[]{:S(2)}, u32[]{:S(2)}) collective-permute-start(s16[720,1408]{1,0:T(8,128)(2,1)} %get-tuple-element.232), channel_id=1, source_target_pairs={{4,1},{6,3},{9,12},{11,14},{20,17},{22,19},{25,28},{27,30}} | collective-permute-start | bytes 6082568 | tf_op jit(solution)/shard_map/ppermute | solution.py:446
  160.8 66.0 %collective-permute-start.16 = (s16[720,1408]{1,0:T(8,128)(2,1)}, s16[720,1408]{1,0:T(8,128)(2,1)}, u32[]{:S(2)}, u32[]{:S(2)}) collective-permute-start(s16[720,1408]{1,0:T(8,128)(2,1)} %get-tuple-element.232), channel_id=1, source_target_pairs={{5,1},{7,3},{8,12},{10,14},{21,17},{23,19},{24,28},{26,30}} | collective-permute-start | bytes 6082568 | tf_op jit(solution)/shard_map/ppermute | solution.py:446
  226.8 6.0 %collective-permute-start.19 = (bf16[768,2048]{1,0:T(8,128)(2,1)}, bf16[768,2048]{1,0:T(8,128)(2,1)}, u32[]{:S(2)}, u32[]{:S(2)}) collective-permute-start(bf16[768,2048]{1,0:T(8,128)(2,1)} %collective-permute-done.12.refs_10_.refs_8_.refs_14_), channel_id=1, source_target_pairs={{0,1},{1,0},{2,3},{3,2},{4,5},{5,4},{6,7},{7,6},{8,9},{9,8},{10,11... | collective-permute-start | bytes 9437192 | tf_op jit(solution)/shard_map/ppermute | solution.py:446
  226.8 10.5 %collective-permute-start.18 = (bf16[768,2048]{1,0:T(8,128)(2,1)}, bf16[768,2048]{1,0:T(8,128)(2,1)}, u32[]{:S(2)}, u32[]{:S(2)}) collective-permute-start(bf16[768,2048]{1,0:T(8,128)(2,1)} %collective-permute-done.11.refs_2_.refs_8_), channel_id=1, source_target_pairs={{0,1},{1,0},{2,3},{3,2},{4,5},{5,4},{6,7},{7,6},{8,9},{9,8},{10,11... | collective-permute-start | bytes 9437192 | tf_op jit(solution)/shard_map/ppermute | solution.py:446
  227.3 33.4 %collective-permute-start.21 = (bf16[640,2048]{1,0:T(8,128)(2,1)}, bf16[640,2048]{1,0:T(8,128)(2,1)}, u32[]{:S(2)}, u32[]{:S(2)}) collective-permute-start(bf16[640,2048]{1,0:T(8,128)(2,1)} %collective-permute-done.2.refs_8_.refs_2_.refs_4_), channel_id=1, source_target_pairs={{4,8},{5,9},{6,10},{7,11},{8,4},{9,5},{10,6},{11,7},{20,24},{21,25... | collective-permute-start | bytes 7864328 | tf_op jit(solution)/shard_map/ppermute | solution.py:446
  229.4 25.1 %collective-permute-start.23 = (s16[336,1408]{1,0:T(8,128)(2,1)}, s16[336,1408]{1,0:T(8,128)(2,1)S(1)}, u32[]{:S(2)}, u32[]{:S(2)}) collective-permute-start(s16[336,1408]{1,0:T(8,128)(2,1)} %get-tuple-element.251), channel_id=1, source_target_pairs={{4,1},{6,3},{9,12},{11,14},{20,17},{22,19},{25,28},{27,30}} | collective-permute-start | bytes 2838536 | tf_op jit(solution)/shard_map/ppermute | solution.py:446
  230.7 24.5 %collective-permute-start.22 = (s16[336,1408]{1,0:T(8,128)(2,1)}, s16[336,1408]{1,0:T(8,128)(2,1)}, u32[]{:S(2)}, u32[]{:S(2)}) collective-permute-start(s16[336,1408]{1,0:T(8,128)(2,1)} %get-tuple-element.251), channel_id=1, source_target_pairs={{5,1},{7,3},{8,12},{10,14},{21,17},{23,19},{24,28},{26,30}} | collective-permute-start | bytes 2838536 | tf_op jit(solution)/shard_map/ppermute | solution.py:446
  254.5 6.2 %copy-start.4 = (s16[336,1408]{1,0:T(8,128)(2,1)}, s16[336,1408]{1,0:T(8,128)(2,1)S(1)}, u32[]{:S(2)}) copy-start(s16[336,1408]{1,0:T(8,128)(2,1)S(1)} %collective-permute-done.23.refs_2_) | copy-start | bytes 2838532
  255.2 28.9 %collective-permute-start.25 = (s16[400,1408]{1,0:T(8,128)(2,1)}, s16[400,1408]{1,0:T(8,128)(2,1)}, u32[]{:S(2)}, u32[]{:S(2)}) collective-permute-start(s16[400,1408]{1,0:T(8,128)(2,1)} %get-tuple-element.261), channel_id=1, source_target_pairs={{4,1},{6,3},{9,12},{11,14},{20,17},{22,19},{25,28},{27,30}} | collective-permute-start | bytes 3379208 | tf_op jit(solution)/shard_map/ppermute | solution.py:446
  256.5 28.3 %collective-permute-start.24 = (s16[400,1408]{1,0:T(8,128)(2,1)}, s16[400,1408]{1,0:T(8,128)(2,1)}, u32[]{:S(2)}, u32[]{:S(2)}) collective-permute-start(s16[400,1408]{1,0:T(8,128)(2,1)} %get-tuple-element.261), channel_id=1, source_target_pairs={{5,1},{7,3},{8,12},{10,14},{21,17},{23,19},{24,28},{26,30}} | collective-permute-start | bytes 3379208 | tf_op jit(solution)/shard_map/ppermute | solution.py:446
  257.8 81.5 %collective-permute-start.20 = (bf16[768,2048]{1,0:T(8,128)(2,1)}, bf16[768,2048]{1,0:T(8,128)(2,1)}, u32[]{:S(2)}, u32[]{:S(2)}) collective-permute-start(bf16[768,2048]{1,0:T(8,128)(2,1)} %bitcast_multiply_fusion.refs_4_.refs_8_.refs_6_.refs_12_), channel_id=1, source_target_pairs={{0,2},{1,3},{2,0},{3,1},{4,6},{5,7},{6,4},{7,5},{8,10},{9,11},{10,... | collective-permute-start | bytes 9437192 | tf_op jit(solution)/shard_map/ppermute | solution.py:446
  284.8 5.3 %collective-permute-start.26 = (bf16[640,2048]{1,0:T(8,128)(2,1)}, bf16[640,2048]{1,0:T(8,128)(2,1)}, u32[]{:S(2)}, u32[]{:S(2)}) collective-permute-start(bf16[640,2048]{1,0:T(8,128)(2,1)} %collective-permute-done.21.refs_10_.refs_8_.refs_18_), channel_id=1, source_target_pairs={{0,1},{1,0},{2,3},{3,2},{4,5},{5,4},{6,7},{7,6},{8,9},{9,8},{10,11... | collective-permute-start | bytes 7864328 | tf_op jit(solution)/shard_map/ppermute | solution.py:446
  284.8 51.3 %collective-permute-start.28 = (s16[1424,768]{1,0:T(8,128)(2,1)}, s16[1424,768]{1,0:T(8,128)(2,1)}, u32[]{:S(2)}, u32[]{:S(2)}) collective-permute-start(s16[1424,768]{1,0:T(8,128)(2,1)} %get-tuple-element.273), channel_id=1, source_target_pairs={{4,1},{6,3},{9,12},{11,14},{20,17},{22,19},{25,28},{27,30}} | collective-permute-start | bytes 6561800 | tf_op jit(solution)/shard_map/ppermute | solution.py:446
  286.1 51.8 %collective-permute-start.27 = (s16[1424,768]{1,0:T(8,128)(2,1)}, s16[1424,768]{1,0:T(8,128)(2,1)}, u32[]{:S(2)}, u32[]{:S(2)}) collective-permute-start(s16[1424,768]{1,0:T(8,128)(2,1)} %get-tuple-element.273), channel_id=1, source_target_pairs={{5,1},{7,3},{8,12},{10,14},{21,17},{23,19},{24,28},{26,30}} | collective-permute-start | bytes 6561800 | tf_op jit(solution)/shard_map/ppermute | solution.py:446
  338.0 44.2 %collective-permute-start.30 = (s16[2848,640]{1,0:T(8,128)(2,1)}, s16[2848,640]{1,0:T(8,128)(2,1)}, u32[]{:S(2)}, u32[]{:S(2)}) collective-permute-start(s16[2848,640]{1,0:T(8,128)(2,1)} %get-tuple-element.308), channel_id=1, source_target_pairs={{4,1},{6,3},{9,12},{11,14},{20,17},{22,19},{25,28},{27,30}} | collective-permute-start | bytes 10936328 | tf_op jit(solution)/shard_map/ppermute | solution.py:446
  339.2 25.1 %collective-permute-start.29 = (bf16[768,2048]{1,0:T(8,128)(2,1)}, bf16[768,2048]{1,0:T(8,128)(2,1)}, u32[]{:S(2)}, u32[]{:S(2)}) collective-permute-start(bf16[768,2048]{1,0:T(8,128)(2,1)} %collective-permute-done.20.refs_2_), channel_id=1, source_target_pairs={{0,1},{1,0},{2,3},{3,2},{4,5},{5,4},{6,7},{7,6},{8,9},{9,8},{10,11... | collective-permute-start | bytes 9437192 | tf_op jit(solution)/shard_map/ppermute | solution.py:446
where the time goes:
time: 397 us; the launch traced here: 390 us
  waiting for transfers between devices  290 us (73%)
  Pallas kernels  53.2 us (13%)
  starting transfers between devices  36.8 us (9%)
  other arithmetic  7.39 us (2%)
    ppermute x31, waiting for transfers between devices, permute(): return lax.ppermute(value, AXES, pairs)  290 us
    ppermute x31, starting transfers between devices, permute(): return lax.ppermute(value, AXES, pairs)  36.8 us
    pallas_call x5, Pallas kernels, decode_call(): pl.pallas_call(functools.partial(decode_kernel, blocks, pieces), out_shap...  32.5 us
    pallas_call x12, Pallas kernels, mm_call(): pl.pallas_call(functools.partial(mm_kernel, send, active, blocks, pieces,...  20.8 us
  transfers between devices with their start and end apart: 31, of which 22 were waited for; matrix products, arithmetic and copies ran while one was open for 0% of the time, Pallas kernels for 12%

commit v1 on v0

--- a/solution.py
+++ b/solution.py
@@ -91,8 +91,8 @@
     return out.at[a, pl.ds(lo, count), pl.ds(base, width)]
 
 
-def groups_of(send, blocks, pieces):
-    if not send and len(blocks) == 1:
+def groups_of(blocks, pieces):
+    if len(blocks) == 1:
         return [(0, [p]) for p in range(len(pieces))]
     return [(b, list(range(len(pieces)))) for b in range(len(blocks))]
 
@@ -116,7 +116,7 @@
     begins = locals_of(pieces)
     firsts = [sum(r.mine for r in blocks[:b]) for b in range(len(blocks))]
     total = sum(r.mine for r in blocks)
-    groups = groups_of(send, blocks, pieces)
+    groups = groups_of(blocks, pieces)
     token[...] = jnp.zeros_like(token)
 
     def col_copy(p, aux, core):
@@ -156,8 +156,10 @@
         b, members = groups[g]
         r = blocks[b]
         if send:
-            where = out.at[pl.ds(firsts[b] + i * r.tile, r.tile), :]
-            return [pltpu.make_async_copy(obuf.at[slot, pl.ds(0, r.tile), :], where, osem.at[slot, 0])]
+            held = sum(pieces[p][2] for p in members)
+            where = out.at[pl.ds(firsts[b] + i * r.tile, r.tile), pl.ds(begins[members[0]], held)]
+            source = obuf.at[slot, pl.ds(0, r.tile), pl.ds(0, held)]
+            return [pltpu.make_async_copy(source, where, osem.at[slot, 0])]
         made = []
         for p in members:
             second, off, n = pieces[p]
@@ -238,9 +240,9 @@
             load(p)
         if send:
             ebuf[...] = jnp.zeros_like(ebuf)
-        scales = 0
         for g, (b, members) in enumerate(groups):
             r = blocks[b]
+            scales = sum(other.mine // other.group for other in blocks[:b])
             new_rows = g == 0 or groups[g - 1][0] != b
             new_cols = [p for p in members if all(p not in group[1] for group in groups[:g])]
 
@@ -282,7 +284,6 @@
                 return carry
 
             lax.fori_loop(0, r.steps, body, 0)
-            scales += r.mine // r.group
         if send:
             ecode[...] = ebuf[...].astype(jnp.int32).astype(jnp.int16)
             exp_copy().start()
@@ -297,7 +298,7 @@
     depth = row_arrays[0][0][2][0][0].shape[1]
     total = sum(r.mine for r in blocks)
     tile = max(r.tile for r in blocks)
-    held = max(sum(pieces[p][2] for p in ps) for _, ps in groups_of(send, blocks, pieces))
+    held = max(sum(pieces[p][2] for p in ps) for _, ps in groups_of(blocks, pieces))
     anywhere = pl.BlockSpec(memory_space=pltpu.HBM)
     operands = [flags, token]
     row_layout, col_layout = [], []

time: 397 us -> 394 us (level)
  no operation moved by 1% of the time
where the time goes in v1:
time: 394 us; the launch traced here: 387 us
  waiting for transfers between devices  288 us (73%)
  Pallas kernels  53.4 us (14%)
  starting transfers between devices  36.7 us (9%)
  other arithmetic  7.39 us (2%)
    ppermute x31, waiting for transfers between devices, permute(): return lax.ppermute(value, AXES, pairs)  288 us
    ppermute x31, starting transfers between devices, permute(): return lax.ppermute(value, AXES, pairs)  36.7 us
    pallas_call x5, Pallas kernels, decode_call(): pl.pallas_call(functools.partial(decode_kernel, blocks, pieces), out_shap...  32.5 us
    pallas_call x12, Pallas kernels, mm_call(): pl.pallas_call(functools.partial(mm_kernel, send, active, blocks, pieces,...  20.9 us
  transfers between devices with their start and end apart: 31, of which 22 were waited for; matrix products, arithmetic and copies ran while one was open for 0% of the time, Pallas kernels for 12%

profile of v1, /device:TPU:1, one launch (start us, length us, event | category | flops | bytes accessed | tf_op | source)
XLA Modules:
  0.0 387.2 jit_solution(6054700991006028340)
XLA Ops:
  0.9 2.0 bitcast_multiply_fusion.1.refs_2_.refs_6_.refs_4_.refs_16_
  3.0 4.7 %bitcast_multiply_fusion.refs_4_.refs_8_.refs_6_.refs_12_ = bf16[768,2048]{1,0:T(8,128)(2,1)} fusion(bf16[1,1408,2048]{2,1,0:T(8,128)(2,1)} %param.2, bf16[768]{0:T(1024)(128)(2,1)S(1)} %broadcast_bitcast_fusion.1), kind=kLoop, calls=%fused_computation | loop fusion | flops 1572864 | bytes 6292992 | tf_op jit(solution)/shard_map/mul | solution.py:484
  8.1 2.3 collective-permute-start.2
  10.4 2.1 collective-permute-start.1
  13.8 3.1 collective-permute-done.4.refs_3_.refs_7_.refs_5_.refs_17_
  17.3 50.1 %collective-permute-done.2.refs_8_.refs_2_.refs_4_ = bf16[640,2048]{1,0:T(8,128)(2,1)} collective-permute-done((bf16[640,2048]{1,0:T(8,128)(2,1)S(1)}, bf16[640,2048]{1,0:T(8,128)(2,1)}, u32[]{:S(2)}, u32[]{:S(2)}) %collective-permute-start.2) | collective-permute-done | bytes 2621472 | tf_op jit(solution)/shard_map/ppermute | solution.py:447
  67.3 2.8 collective-permute-done.refs_6_.refs_2_
  70.2 1.7 collective-permute-start.8
  71.9 2.5 collective-permute-start.5
  74.3 2.3 collective-permute-start.10
  77.2 2.1 collective-permute-start.9
  79.9 4.0 %collective-permute-done.7.refs_11_.refs_7_.refs_5_ = bf16[640,2048]{1,0:T(8,128)(2,1)} collective-permute-done((bf16[640,2048]{1,0:T(8,128)(2,1)}, bf16[640,2048]{1,0:T(8,128)(2,1)}, u32[]{:S(2)}, u32[]{:S(2)}) %collective-permute-start.7) | collective-permute-done | bytes 2621472 | tf_op jit(solution)/shard_map/ppermute | solution.py:447
  83.9 1.5 collective-permute-done.6.refs_7_.refs_3_
  86.0 1.9 result_tiles.7
  87.9 1.6 result_tiles.8
  89.5 53.5 %collective-permute-done.5.refs_4_.refs_8_ = bf16[768,2048]{1,0:T(8,128)(2,1)} collective-permute-done((bf16[768,2048]{1,0:T(8,128)(2,1)}, bf16[768,2048]{1,0:T(8,128)(2,1)}, u32[]{:S(2)}, u32[]{:S(2)}) %collective-permute-start.5) | collective-permute-done | bytes 3145760 | tf_op jit(solution)/shard_map/ppermute | solution.py:447
  144.2 2.4 collective-permute-start.12
  146.6 2.3 collective-permute-start.11
  149.3 4.5 %collective-permute-done.14.refs_9_.refs_7_.refs_11_ = bf16[768,2048]{1,0:T(8,128)(2,1)} collective-permute-done((bf16[768,2048]{1,0:T(8,128)(2,1)}, bf16[768,2048]{1,0:T(8,128)(2,1)}, u32[]{:S(2)}, u32[]{:S(2)}) %collective-permute-start.14) | collective-permute-done | bytes 3145760 | tf_op jit(solution)/shard_map/ppermute | solution.py:447
  153.8 3.7 collective-permute-done.13.refs_3_.refs_7_
  157.6 2.0 coded_tiles.5
  159.5 1.3 collective-permute-start.17
  160.8 1.3 collective-permute-start.16
  162.1 1.5 coded_tiles.6
  163.6 1.9 result_tiles.9
  165.5 56.9 %collective-permute-done.17.refs_2_ = s16[720,1408]{1,0:T(8,128)(2,1)} collective-permute-done((s16[720,1408]{1,0:T(8,128)(2,1)}, s16[720,1408]{1,0:T(8,128)(2,1)}, u32[]{:S(2)}, u32[]{:S(2)}) %collective-permute-start.17) | collective-permute-done | bytes 2027552 | tf_op jit(solution)/shard_map/ppermute | solution.py:447
  222.4 1.4 collective-permute-done.16.refs_3_
  224.4 2.1 collective-permute-start.21
  229.9 4.5 %collective-permute-done.18.refs_3_.refs_9_ = bf16[768,2048]{1,0:T(8,128)(2,1)} collective-permute-done((bf16[768,2048]{1,0:T(8,128)(2,1)}, bf16[768,2048]{1,0:T(8,128)(2,1)}, u32[]{:S(2)}, u32[]{:S(2)}) %collective-permute-start.18) | collective-permute-done | bytes 3145760 | tf_op jit(solution)/shard_map/ppermute | solution.py:447
  234.4 1.7 coded_tiles.7
  236.0 15.5 %collective-permute-done.23.refs_2_ = s16[336,1408]{1,0:T(8,128)(2,1)S(1)} collective-permute-done((s16[336,1408]{1,0:T(8,128)(2,1)}, s16[336,1408]{1,0:T(8,128)(2,1)S(1)}, u32[]{:S(2)}, u32[]{:S(2)}) %collective-permute-start.23) | collective-permute-done | bytes 946208 | tf_op jit(solution)/shard_map/ppermute | solution.py:447
  253.5 1.3 collective-permute-start.24
  256.1 1.6 coded_tiles.8
  257.8 23.4 %collective-permute-done.25.refs_2_ = s16[400,1408]{1,0:T(8,128)(2,1)} collective-permute-done((s16[400,1408]{1,0:T(8,128)(2,1)}, s16[400,1408]{1,0:T(8,128)(2,1)}, u32[]{:S(2)}, u32[]{:S(2)}) %collective-permute-start.25) | collective-permute-done | bytes 1126432 | tf_op jit(solution)/shard_map/ppermute | solution.py:447
  284.5 2.7 collective-permute-done.26.refs_11_.refs_9_.refs_19_
  287.1 1.9 coded_tiles.9
  289.0 1.7 result_tiles.10
  290.7 1.9 result_tiles.11
  292.6 1.9 result_tiles.12
  294.5 38.7 %collective-permute-done.28.refs_2_ = s16[1424,768]{1,0:T(8,128)(2,1)} collective-permute-done((s16[1424,768]{1,0:T(8,128)(2,1)}, s16[1424,768]{1,0:T(8,128)(2,1)}, u32[]{:S(2)}, u32[]{:S(2)}) %collective-permute-start.28) | collective-permute-done | bytes 2187296 | tf_op jit(solution)/shard_map/ppermute | solution.py:447
  333.1 1.9 collective-permute-done.27.refs_3_
  336.4 7.0 %decode_tiles.5 = (f32[2,1408,2816]{2,1,0:T(8,128)}, f32[8,128]{1,0:T(8,128)}) custom-call(s32[10]{0:T(128)} %stack.67.refs_0_, f32[8,128]{1,0:T(8,128)} %get-tuple-element.286.refs_1_, s16[720,1408]{1,0:T(8,128)(2,1)} %collective-permute-done.17.refs_2_, s16[720,1408]{1,0:T(8,128)(2,1)} %collective-permute-done.16.refs_3_, ...), custom_call_target="tpu_custom_call", output_to_operand_aliasing={{0}: (4, {})} | custom-call | flops 1 | bytes 1 | tf_op jit(solution)/shard_map/decode_tiles/pallas_call | solution.py:416
  343.4 4.9 %decode_tiles.6 = (f32[2,1408,2816]{2,1,0:T(8,128)}, f32[8,128]{1,0:T(8,128)}) custom-call(s32[10]{0:T(128)} %stack.67.refs_0_, f32[8,128]{1,0:T(8,128)} %get-tuple-element.290.refs_1_, s16[336,1408]{1,0:T(8,128)(2,1)} %copy-done.4, s16[336,1408]{1,0:T(8,128)(2,1)} %collective-permute-done.22.refs_3_, ...), custom_call_target="tpu_custom_call", output_to_operand_aliasing={{0}: (4, {})} | custom-call | flops 1 | bytes 1 | tf_op jit(solution)/shard_map/decode_tiles/pallas_call | solution.py:416
  348.3 5.2 %decode_tiles.7 = (f32[2,1408,2816]{2,1,0:T(8,128)}, f32[8,128]{1,0:T(8,128)}) custom-call(s32[10]{0:T(128)} %stack.67.refs_0_, f32[8,128]{1,0:T(8,128)} %get-tuple-element.294.refs_1_, s16[400,1408]{1,0:T(8,128)(2,1)} %collective-permute-done.25.refs_2_, s16[400,1408]{1,0:T(8,128)(2,1)} %collective-permute-done.24.refs_3_, ...), custom_call_target="tpu_custom_call", output_to_operand_aliasing={{0}: (4, {})} | custom-call | flops 1 | bytes 1 | tf_op jit(solution)/shard_map/decode_tiles/pallas_call | solution.py:416
  353.5 8.0 %decode_tiles.8 = (f32[2,1408,2816]{2,1,0:T(8,128)}, f32[8,128]{1,0:T(8,128)}) custom-call(s32[10]{0:T(128)} %stack.67.refs_0_, f32[8,128]{1,0:T(8,128)} %get-tuple-element.298.refs_1_, s16[1424,768]{1,0:T(8,128)(2,1)} %collective-permute-done.28.refs_2_, s16[1424,768]{1,0:T(8,128)(2,1)} %collective-permute-done.27.refs_3_, ...), custom_call_target="tpu_custom_call", output_to_operand_aliasing={{0}: (4, {})} | custom-call | flops 1 | bytes 1 | tf_op jit(solution)/shard_map/decode_tiles/pallas_call | solution.py:416
  361.5 1.6 result_tiles.13
  363.1 16.2 %collective-permute-done.30.refs_2_ = s16[2848,640]{1,0:T(8,128)(2,1)} collective-permute-done((s16[2848,640]{1,0:T(8,128)(2,1)}, s16[2848,640]{1,0:T(8,128)(2,1)}, u32[]{:S(2)}, u32[]{:S(2)}) %collective-permute-start.30) | collective-permute-done | bytes 3645472 | tf_op jit(solution)/shard_map/ppermute | solution.py:447
  379.3 7.4 %decode_tiles.9 = (f32[2,1408,2816]{2,1,0:T(8,128)}, f32[8,128]{1,0:T(8,128)}) custom-call(s32[10]{0:T(128)} %stack.67.refs_0_, f32[8,128]{1,0:T(8,128)} %get-tuple-element.307.refs_1_, s16[2848,640]{1,0:T(8,128)(2,1)} %collective-permute-done.30.refs_2_, f32[2,1408,2816]{2,1,0:T(8,128)} %get-tuple-element.309.refs_3_), custom_call_target="tpu_custom_call", output_to_operand_aliasing={{0}: (3, {})} | custom-call | flops 1 | bytes 1 | tf_op jit(solution)/shard_map/decode_tiles/pallas_call | solution.py:416
  (50 shorter events, 18.2 us)
Async XLA Ops:
  2.9 9.7 %copy-start = (bf16[640,2048]{1,0:T(8,128)(2,1)}, bf16[640,2048]{1,0:T(8,128)(2,1)S(1)}, u32[]{:S(2)}) copy-start(bf16[640,2048]{1,0:T(8,128)(2,1)S(1)} %bitcast_multiply_fusion.1.refs_2_.refs_6_.refs_4_.refs_16_) | copy-start | bytes 7864324
  7.6 9.6 %collective-permute-start.3 = (bf16[768,2048]{1,0:T(8,128)(2,1)}, bf16[768,2048]{1,0:T(8,128)(2,1)S(1)}, u32[]{:S(2)}, u32[]{:S(2)}) collective-permute-start(bf16[768,2048]{1,0:T(8,128)(2,1)} %bitcast_multiply_fusion.refs_4_.refs_8_.refs_6_.refs_12_), channel_id=1, source_target_pairs={{0,1},{1,0},{2,3},{3,2},{4,5},{5,4},{6,7},{7,6},{8,9},{9,8},{10,11... | collective-permute-start | bytes 9437192 | tf_op jit(solution)/shard_map/ppermute | solution.py:447
  7.7 9.2 %collective-permute-start.4 = (bf16[640,2048]{1,0:T(8,128)(2,1)S(1)}, bf16[640,2048]{1,0:T(8,128)(2,1)S(1)}, u32[]{:S(2)}, u32[]{:S(2)}) collective-permute-start(bf16[640,2048]{1,0:T(8,128)(2,1)S(1)} %bitcast_multiply_fusion.1.refs_2_.refs_6_.refs_4_.refs_16_), channel_id=1, source_target_pairs={{0,1},{1,0},{2,3},{3,2},{4,5},{5,4},{6,7},{7,6},{8,9},{9,8},{10,11... | collective-permute-start | bytes 7864328 | tf_op jit(solution)/shard_map/ppermute | solution.py:447
  8.1 59.2 %collective-permute-start.2 = (bf16[640,2048]{1,0:T(8,128)(2,1)S(1)}, bf16[640,2048]{1,0:T(8,128)(2,1)}, u32[]{:S(2)}, u32[]{:S(2)}) collective-permute-start(bf16[640,2048]{1,0:T(8,128)(2,1)S(1)} %bitcast_multiply_fusion.1.refs_2_.refs_6_.refs_4_.refs_16_), channel_id=1, source_target_pairs={{0,4},{1,5},{2,6},{3,7},{4,0},{5,1},{6,2},{7,3},{8,12},{9,13},{10,... | collective-permute-start | bytes 7864328 | tf_op jit(solution)/shard_map/ppermute | solution.py:447
  10.4 56.9 %collective-permute-start.1 = (bf16[640,2048]{1,0:T(8,128)(2,1)S(1)}, bf16[640,2048]{1,0:T(8,128)(2,1)}, u32[]{:S(2)}, u32[]{:S(2)}) collective-permute-start(bf16[640,2048]{1,0:T(8,128)(2,1)S(1)} %bitcast_multiply_fusion.1.refs_2_.refs_6_.refs_4_.refs_16_), channel_id=1, source_target_pairs={{4,8},{5,9},{6,10},{7,11},{8,4},{9,5},{10,6},{11,7},{20,24},{21,25... | collective-permute-start | bytes 7864328 | tf_op jit(solution)/shard_map/ppermute | solution.py:447
  12.6 57.6 %collective-permute-start = (bf16[640,2048]{1,0:T(8,128)(2,1)S(1)}, bf16[640,2048]{1,0:T(8,128)(2,1)S(1)}, u32[]{:S(2)}, u32[]{:S(2)}) collective-permute-start(bf16[640,2048]{1,0:T(8,128)(2,1)S(1)} %bitcast_multiply_fusion.1.refs_2_.refs_6_.refs_4_.refs_16_), channel_id=1, source_target_pairs={{0,2},{1,3},{2,0},{3,1},{4,6},{5,7},{6,4},{7,5},{8,10},{9,11},{10,... | collective-permute-start | bytes 7864328 | tf_op jit(solution)/shard_map/ppermute | solution.py:447
  16.9 55.0 %copy-start.2 = (bf16[640,2048]{1,0:T(8,128)(2,1)}, bf16[640,2048]{1,0:T(8,128)(2,1)S(1)}, u32[]{:S(2)}) copy-start(bf16[640,2048]{1,0:T(8,128)(2,1)S(1)} %collective-permute-done.4.refs_3_.refs_7_.refs_5_.refs_17_) | copy-start | bytes 7864324
  17.3 52.9 %copy-start.1 = (bf16[768,2048]{1,0:T(8,128)(2,1)}, bf16[768,2048]{1,0:T(8,128)(2,1)S(1)}, u32[]{:S(2)}) copy-start(bf16[768,2048]{1,0:T(8,128)(2,1)S(1)} %collective-permute-done.3.refs_5_.refs_9_.refs_7_.refs_13_) | copy-start | bytes 9437188
  70.2 6.8 %copy-start.3 = (bf16[640,2048]{1,0:T(8,128)(2,1)}, bf16[640,2048]{1,0:T(8,128)(2,1)S(1)}, u32[]{:S(2)}) copy-start(bf16[640,2048]{1,0:T(8,128)(2,1)S(1)} %collective-permute-done.refs_6_.refs_2_) | copy-start | bytes 7864324
  70.2 7.0 %collective-permute-start.8 = (bf16[640,2048]{1,0:T(8,128)(2,1)}, bf16[640,2048]{1,0:T(8,128)(2,1)}, u32[]{:S(2)}, u32[]{:S(2)}) collective-permute-start(bf16[640,2048]{1,0:T(8,128)(2,1)} %collective-permute-done.2.refs_8_.refs_2_.refs_4_), channel_id=1, source_target_pairs={{0,1},{1,0},{2,3},{3,2},{4,5},{5,4},{6,7},{7,6},{8,9},{9,8},{10,11... | collective-permute-start | bytes 7864328 | tf_op jit(solution)/shard_map/ppermute | solution.py:447
  71.9 71.2 %collective-permute-start.5 = (bf16[768,2048]{1,0:T(8,128)(2,1)}, bf16[768,2048]{1,0:T(8,128)(2,1)}, u32[]{:S(2)}, u32[]{:S(2)}) collective-permute-start(bf16[768,2048]{1,0:T(8,128)(2,1)} %bitcast_multiply_fusion.refs_4_.refs_8_.refs_6_.refs_12_), channel_id=1, source_target_pairs={{0,4},{1,5},{2,6},{3,7},{4,0},{5,1},{6,2},{7,3},{8,12},{9,13},{10,... | collective-permute-start | bytes 9437192 | tf_op jit(solution)/shard_map/ppermute | solution.py:447
  74.3 68.7 %collective-permute-start.10 = (bf16[768,2048]{1,0:T(8,128)(2,1)}, bf16[768,2048]{1,0:T(8,128)(2,1)}, u32[]{:S(2)}, u32[]{:S(2)}) collective-permute-start(bf16[768,2048]{1,0:T(8,128)(2,1)} %bitcast_multiply_fusion.refs_4_.refs_8_.refs_6_.refs_12_), channel_id=1, source_target_pairs={{4,8},{5,9},{6,10},{7,11},{8,4},{9,5},{10,6},{11,7},{20,24},{21,25... | collective-permute-start | bytes 9437192 | tf_op jit(solution)/shard_map/ppermute | solution.py:447
  76.6 7.3 %collective-permute-start.7 = (bf16[640,2048]{1,0:T(8,128)(2,1)}, bf16[640,2048]{1,0:T(8,128)(2,1)}, u32[]{:S(2)}, u32[]{:S(2)}) collective-permute-start(bf16[640,2048]{1,0:T(8,128)(2,1)} %collective-permute-done.1.refs_10_.refs_6_.refs_4_), channel_id=1, source_target_pairs={{0,1},{1,0},{2,3},{3,2},{4,5},{5,4},{6,7},{7,6},{8,9},{9,8},{10,11... | collective-permute-start | bytes 7864328 | tf_op jit(solution)/shard_map/ppermute | solution.py:447
  77.0 8.4 %collective-permute-start.6 = (bf16[640,2048]{1,0:T(8,128)(2,1)S(1)}, bf16[640,2048]{1,0:T(8,128)(2,1)}, u32[]{:S(2)}, u32[]{:S(2)}) collective-permute-start(bf16[640,2048]{1,0:T(8,128)(2,1)S(1)} %collective-permute-done.refs_6_.refs_2_), channel_id=1, source_target_pairs={{0,1},{1,0},{2,3},{3,2},{4,5},{5,4},{6,7},{7,6},{8,9},{9,8},{10,11... | collective-permute-start | bytes 7864328 | tf_op jit(solution)/shard_map/ppermute | solution.py:447
  77.2 65.9 %collective-permute-start.9 = (bf16[640,2048]{1,0:T(8,128)(2,1)}, bf16[640,2048]{1,0:T(8,128)(2,1)}, u32[]{:S(2)}, u32[]{:S(2)}) collective-permute-start(bf16[640,2048]{1,0:T(8,128)(2,1)} %collective-permute-done.2.refs_8_.refs_2_.refs_4_), channel_id=1, source_target_pairs={{4,6},{5,7},{6,4},{7,5},{8,10},{9,11},{10,8},{11,9},{20,22},{21,23... | collective-permute-start | bytes 7864328 | tf_op jit(solution)/shard_map/ppermute | solution.py:447
  143.0 6.3 %collective-permute-start.15 = (bf16[768,2048]{1,0:T(8,128)(2,1)}, bf16[768,2048]{1,0:T(8,128)(2,1)}, u32[]{:S(2)}, u32[]{:S(2)}) collective-permute-start(bf16[768,2048]{1,0:T(8,128)(2,1)} %collective-permute-done.5.refs_4_.refs_8_), channel_id=1, source_target_pairs={{0,1},{1,0},{2,3},{3,2},{4,5},{5,4},{6,7},{7,6},{8,9},{9,8},{10,11... | collective-permute-start | bytes 9437192 | tf_op jit(solution)/shard_map/ppermute | solution.py:447
  143.7 10.1 %collective-permute-start.14 = (bf16[768,2048]{1,0:T(8,128)(2,1)}, bf16[768,2048]{1,0:T(8,128)(2,1)}, u32[]{:S(2)}, u32[]{:S(2)}) collective-permute-start(bf16[768,2048]{1,0:T(8,128)(2,1)} %collective-permute-done.10.refs_8_.refs_6_.refs_10_), channel_id=1, source_target_pairs={{0,1},{1,0},{2,3},{3,2},{4,5},{5,4},{6,7},{7,6},{8,9},{9,8},{10,11... | collective-permute-start | bytes 9437192 | tf_op jit(solution)/shard_map/ppermute | solution.py:447
  143.8 13.8 %collective-permute-start.13 = (bf16[640,2048]{1,0:T(8,128)(2,1)}, bf16[640,2048]{1,0:T(8,128)(2,1)}, u32[]{:S(2)}, u32[]{:S(2)}) collective-permute-start(bf16[640,2048]{1,0:T(8,128)(2,1)} %collective-permute-done.9.refs_2_.refs_6_), channel_id=1, source_target_pairs={{0,1},{1,0},{2,3},{3,2},{4,5},{5,4},{6,7},{7,6},{8,9},{9,8},{10,11... | collective-permute-start | bytes 7864328 | tf_op jit(solution)/shard_map/ppermute | solution.py:447
  144.2 21.3 %collective-permute-start.12 = (bf16[768,2048]{1,0:T(8,128)(2,1)}, bf16[768,2048]{1,0:T(8,128)(2,1)}, u32[]{:S(2)}, u32[]{:S(2)}) collective-permute-start(bf16[768,2048]{1,0:T(8,128)(2,1)} %collective-permute-done.5.refs_4_.refs_8_), channel_id=1, source_target_pairs={{4,8},{5,9},{6,10},{7,11},{8,4},{9,5},{10,6},{11,7},{20,24},{21,25... | collective-permute-start | bytes 9437192 | tf_op jit(solution)/shard_map/ppermute | solution.py:447
  146.6 18.9 %collective-permute-start.11 = (bf16[768,2048]{1,0:T(8,128)(2,1)}, bf16[768,2048]{1,0:T(8,128)(2,1)}, u32[]{:S(2)}, u32[]{:S(2)}) collective-permute-start(bf16[768,2048]{1,0:T(8,128)(2,1)} %collective-permute-done.5.refs_4_.refs_8_), channel_id=1, source_target_pairs={{4,6},{5,7},{6,4},{7,5},{8,10},{9,11},{10,8},{11,9},{20,22},{21,23... | collective-permute-start | bytes 9437192 | tf_op jit(solution)/shard_map/ppermute | solution.py:447
  159.5 62.9 %collective-permute-start.17 = (s16[720,1408]{1,0:T(8,128)(2,1)}, s16[720,1408]{1,0:T(8,128)(2,1)}, u32[]{:S(2)}, u32[]{:S(2)}) collective-permute-start(s16[720,1408]{1,0:T(8,128)(2,1)} %get-tuple-element.232), channel_id=1, source_target_pairs={{4,1},{6,3},{9,12},{11,14},{20,17},{22,19},{25,28},{27,30}} | collective-permute-start | bytes 6082568 | tf_op jit(solution)/shard_map/ppermute | solution.py:447
  160.8 63.0 %collective-permute-start.16 = (s16[720,1408]{1,0:T(8,128)(2,1)}, s16[720,1408]{1,0:T(8,128)(2,1)}, u32[]{:S(2)}, u32[]{:S(2)}) collective-permute-start(s16[720,1408]{1,0:T(8,128)(2,1)} %get-tuple-element.232), channel_id=1, source_target_pairs={{5,1},{7,3},{8,12},{10,14},{21,17},{23,19},{24,28},{26,30}} | collective-permute-start | bytes 6082568 | tf_op jit(solution)/shard_map/ppermute | solution.py:447
  223.9 6.0 %collective-permute-start.19 = (bf16[768,2048]{1,0:T(8,128)(2,1)}, bf16[768,2048]{1,0:T(8,128)(2,1)}, u32[]{:S(2)}, u32[]{:S(2)}) collective-permute-start(bf16[768,2048]{1,0:T(8,128)(2,1)} %collective-permute-done.12.refs_10_.refs_8_.refs_14_), channel_id=1, source_target_pairs={{0,1},{1,0},{2,3},{3,2},{4,5},{5,4},{6,7},{7,6},{8,9},{9,8},{10,11... | collective-permute-start | bytes 9437192 | tf_op jit(solution)/shard_map/ppermute | solution.py:447
  223.9 10.5 %collective-permute-start.18 = (bf16[768,2048]{1,0:T(8,128)(2,1)}, bf16[768,2048]{1,0:T(8,128)(2,1)}, u32[]{:S(2)}, u32[]{:S(2)}) collective-permute-start(bf16[768,2048]{1,0:T(8,128)(2,1)} %collective-permute-done.11.refs_2_.refs_8_), channel_id=1, source_target_pairs={{0,1},{1,0},{2,3},{3,2},{4,5},{5,4},{6,7},{7,6},{8,9},{9,8},{10,11... | collective-permute-start | bytes 9437192 | tf_op jit(solution)/shard_map/ppermute | solution.py:447
  224.4 33.4 %collective-permute-start.21 = (bf16[640,2048]{1,0:T(8,128)(2,1)}, bf16[640,2048]{1,0:T(8,128)(2,1)}, u32[]{:S(2)}, u32[]{:S(2)}) collective-permute-start(bf16[640,2048]{1,0:T(8,128)(2,1)} %collective-permute-done.2.refs_8_.refs_2_.refs_4_), channel_id=1, source_target_pairs={{4,8},{5,9},{6,10},{7,11},{8,4},{9,5},{10,6},{11,7},{20,24},{21,25... | collective-permute-start | bytes 7864328 | tf_op jit(solution)/shard_map/ppermute | solution.py:447
  226.5 25.1 %collective-permute-start.23 = (s16[336,1408]{1,0:T(8,128)(2,1)}, s16[336,1408]{1,0:T(8,128)(2,1)S(1)}, u32[]{:S(2)}, u32[]{:S(2)}) collective-permute-start(s16[336,1408]{1,0:T(8,128)(2,1)} %get-tuple-element.251), channel_id=1, source_target_pairs={{4,1},{6,3},{9,12},{11,14},{20,17},{22,19},{25,28},{27,30}} | collective-permute-start | bytes 2838536 | tf_op jit(solution)/shard_map/ppermute | solution.py:447
  227.8 24.5 %collective-permute-start.22 = (s16[336,1408]{1,0:T(8,128)(2,1)}, s16[336,1408]{1,0:T(8,128)(2,1)}, u32[]{:S(2)}, u32[]{:S(2)}) collective-permute-start(s16[336,1408]{1,0:T(8,128)(2,1)} %get-tuple-element.251), channel_id=1, source_target_pairs={{5,1},{7,3},{8,12},{10,14},{21,17},{23,19},{24,28},{26,30}} | collective-permute-start | bytes 2838536 | tf_op jit(solution)/shard_map/ppermute | solution.py:447
  251.6 6.2 %copy-start.4 = (s16[336,1408]{1,0:T(8,128)(2,1)}, s16[336,1408]{1,0:T(8,128)(2,1)S(1)}, u32[]{:S(2)}) copy-start(s16[336,1408]{1,0:T(8,128)(2,1)S(1)} %collective-permute-done.23.refs_2_) | copy-start | bytes 2838532
  252.3 28.9 %collective-permute-start.25 = (s16[400,1408]{1,0:T(8,128)(2,1)}, s16[400,1408]{1,0:T(8,128)(2,1)}, u32[]{:S(2)}, u32[]{:S(2)}) collective-permute-start(s16[400,1408]{1,0:T(8,128)(2,1)} %get-tuple-element.261), channel_id=1, source_target_pairs={{4,1},{6,3},{9,12},{11,14},{20,17},{22,19},{25,28},{27,30}} | collective-permute-start | bytes 3379208 | tf_op jit(solution)/shard_map/ppermute | solution.py:447
  253.5 28.3 %collective-permute-start.24 = (s16[400,1408]{1,0:T(8,128)(2,1)}, s16[400,1408]{1,0:T(8,128)(2,1)}, u32[]{:S(2)}, u32[]{:S(2)}) collective-permute-start(s16[400,1408]{1,0:T(8,128)(2,1)} %get-tuple-element.261), channel_id=1, source_target_pairs={{5,1},{7,3},{8,12},{10,14},{21,17},{23,19},{24,28},{26,30}} | collective-permute-start | bytes 3379208 | tf_op jit(solution)/shard_map/ppermute | solution.py:447
  254.8 81.5 %collective-permute-start.20 = (bf16[768,2048]{1,0:T(8,128)(2,1)}, bf16[768,2048]{1,0:T(8,128)(2,1)}, u32[]{:S(2)}, u32[]{:S(2)}) collective-permute-start(bf16[768,2048]{1,0:T(8,128)(2,1)} %bitcast_multiply_fusion.refs_4_.refs_8_.refs_6_.refs_12_), channel_id=1, source_target_pairs={{0,2},{1,3},{2,0},{3,1},{4,6},{5,7},{6,4},{7,5},{8,10},{9,11},{10,... | collective-permute-start | bytes 9437192 | tf_op jit(solution)/shard_map/ppermute | solution.py:447
  281.9 5.3 %collective-permute-start.26 = (bf16[640,2048]{1,0:T(8,128)(2,1)}, bf16[640,2048]{1,0:T(8,128)(2,1)}, u32[]{:S(2)}, u32[]{:S(2)}) collective-permute-start(bf16[640,2048]{1,0:T(8,128)(2,1)} %collective-permute-done.21.refs_10_.refs_8_.refs_18_), channel_id=1, source_target_pairs={{0,1},{1,0},{2,3},{3,2},{4,5},{5,4},{6,7},{7,6},{8,9},{9,8},{10,11... | collective-permute-start | bytes 7864328 | tf_op jit(solution)/shard_map/ppermute | solution.py:447
  281.9 51.3 %collective-permute-start.28 = (s16[1424,768]{1,0:T(8,128)(2,1)}, s16[1424,768]{1,0:T(8,128)(2,1)}, u32[]{:S(2)}, u32[]{:S(2)}) collective-permute-start(s16[1424,768]{1,0:T(8,128)(2,1)} %get-tuple-element.273), channel_id=1, source_target_pairs={{4,1},{6,3},{9,12},{11,14},{20,17},{22,19},{25,28},{27,30}} | collective-permute-start | bytes 6561800 | tf_op jit(solution)/shard_map/ppermute | solution.py:447
  283.2 51.8 %collective-permute-start.27 = (s16[1424,768]{1,0:T(8,128)(2,1)}, s16[1424,768]{1,0:T(8,128)(2,1)}, u32[]{:S(2)}, u32[]{:S(2)}) collective-permute-start(s16[1424,768]{1,0:T(8,128)(2,1)} %get-tuple-element.273), channel_id=1, source_target_pairs={{5,1},{7,3},{8,12},{10,14},{21,17},{23,19},{24,28},{26,30}} | collective-permute-start | bytes 6561800 | tf_op jit(solution)/shard_map/ppermute | solution.py:447
  335.0 44.2 %collective-permute-start.30 = (s16[2848,640]{1,0:T(8,128)(2,1)}, s16[2848,640]{1,0:T(8,128)(2,1)}, u32[]{:S(2)}, u32[]{:S(2)}) collective-permute-start(s16[2848,640]{1,0:T(8,128)(2,1)} %get-tuple-element.308), channel_id=1, source_target_pairs={{4,1},{6,3},{9,12},{11,14},{20,17},{22,19},{25,28},{27,30}} | collective-permute-start | bytes 10936328 | tf_op jit(solution)/shard_map/ppermute | solution.py:447
  336.3 25.1 %collective-permute-start.29 = (bf16[768,2048]{1,0:T(8,128)(2,1)}, bf16[768,2048]{1,0:T(8,128)(2,1)}, u32[]{:S(2)}, u32[]{:S(2)}) collective-permute-start(bf16[768,2048]{1,0:T(8,128)(2,1)} %collective-permute-done.20.refs_2_), channel_id=1, source_target_pairs={{0,1},{1,0},{2,3},{3,2},{4,5},{5,4},{6,7},{7,6},{8,9},{9,8},{10,11... | collective-permute-start | bytes 9437192 | tf_op jit(solution)/shard_map/ppermute | solution.py:447
